TPU v7x, 32 devices: a whole 2x2x4 slice. The times are simulated.
32 devices in a mesh: parts: 2 (over y), seq: 4 (over z), chan: 4 (over x, core).
Axes of the slice: x: 2, y: 2, z: 4, core: 2. Of those that a mesh axis runs over, the one named last changes fastest.
Arguments:
- x_tokens: bfloat16 [64, 8192], P(('parts', 'seq'), 'chan'), parts along dimension 0, may hold values from -6 to 6
- norm_gain: float32 [8192], P('chan'), may hold values from 0.5 to 1.5
- w_in: bfloat16 [3, 8192, 8192], P(None, 'seq', 'chan'), may hold values from -0.0625 to 0.0625
- short_filter: float32 [3, 3, 8192], P(None, None, 'seq'), may hold values from -3 to 3
- se_filter: float32 [7, 512], P(None, 'seq'), may hold values from -2 to 2
- w_out: bfloat16 [8192, 8192], P('seq'), may hold values from -0.0625 to 0.0625
Outputs:
- mixed_out: bfloat16 [64, 8192], P(('parts', 'chan'), 'seq'), parts along dimension 0
There are 2 independent parts, one for each index of `parts`. A program takes and returns all parts, laid end to end along the dimension named above; an argument that names none is the same for every part. Nothing has to cross between parts.
All inputs are finite; a program needn't handle non-finite values.
Results may differ from a plain program's by a relative error of at most 0.0086.
Values may be sent and summed in bfloat16 or wider, within the bound.
A program may use at most 128 MiB of HBM per device.

v0:
```python
import jax
import jax.numpy as jnp
from jax import lax
from jax.sharding import PartitionSpec as P

D = 8192
GROUP = 16


epsilon = 1e-06


def from_behind(value, axis, steps):
    count = lax.axis_size(axis)
    leading, last = (max(0, -steps), min(count, count - steps))
    return lax.ppermute(value, axis, [(source, source + steps) for source in range(leading, last)])


def mixer(extended, short_taps, long_taps):
    wide = extended.astype(jnp.float32)
    row_count = wide.shape[0]
    featured = sum(
        (short_taps[offset] * wide[2 - offset : row_count - offset] for offset in range(3))
    )
    queries = featured[:, 0]
    product = featured[:, 1] * featured[:, 2]
    length = product.shape[0]
    filtered = sum(
        (long_taps[offset] * product[6 - offset : length - offset] for offset in range(7))
    )
    return (queries[6:] * filtered).astype(jnp.bfloat16)


def contract_last(left, right):
    return lax.dot_general(
        left, right, (((1,), (1,)), ((), ())), preferred_element_type=jnp.float32
    )


def shards(x_tokens, norm_gain, w_in, short_filter, se_filter, w_out):
    wide = x_tokens.astype(jnp.float32)
    local_squares = jnp.sum(wide * wide, axis=1, keepdims=True)
    total_squares = lax.psum(local_squares, "chan")
    factor = lax.rsqrt(total_squares / D + epsilon)
    normed = (wide * factor * norm_gain).astype(jnp.bfloat16)
    columns = w_in.shape[1]
    flat_in = w_in.reshape(3 * columns, w_in.shape[2])
    piece = lax.all_gather(normed, "seq", axis=0, tiled=True)
    partial_terms = contract_last(piece, flat_in).reshape(piece.shape[0], 3, columns)
    long_full = jnp.repeat(se_filter, GROUP, axis=1)
    mine = lax.psum_scatter(partial_terms, "chan", scatter_dimension=0, tiled=True).astype(
        jnp.bfloat16
    )
    previous = from_behind(mine[-8:], "chan", 1)
    extended = jnp.concatenate([previous, mine], axis=0)
    gated = mixer(extended, short_filter, long_full)
    result = contract_last(lax.all_gather(gated, "seq", axis=1, tiled=True), w_out)
    return result.astype(jnp.bfloat16)


def solution(mesh):
    placed = (
        P(("parts", "seq"), "chan"),
        P("chan"),
        P(None, "seq", "chan"),
        P(None, None, "seq"),
        P(None, "seq"),
        P("seq", None),
    )
    return jax.shard_map(
        shards, mesh=mesh, in_specs=placed, out_specs=P(("parts", "chan"), "seq"), check_vma=False
    )
```

profile of v0, /device:TPU:0, one launch (start us, length us, event | category | flops | bytes accessed | tf_op | source)
XLA Modules:
  0.0 107.6 jit_solution(7954886832939469192)
XLA Ops:
  6.5 0.0 reduce-scatter.2.cloned.1.call-start
  6.5 0.9 fusion.4
  7.4 8.3 %psum.7 = f32[8,1]{0,1:T(1,128)S(1)} all-reduce(f32[8,1]{0,1:T(1,128)S(1)} %bitcast.89), channel_id=1, replica_groups=mesh['parts'=2,'seq'=4,'chan'=4] {'chan'}, use_global_device_ids=true, to_apply=%region_1.0 | all-reduce | flops 8 | bytes 64 | tf_op jit(solution)/shard_map/psum | solution.py:43
  15.8 0.8 fusion.6
  16.6 13.6 %all_gather.6 = bf16[32,2048]{1,0:T(8,128)(2,1)S(1)} all-gather(bf16[8,2048]{1,0:T(8,128)(2,1)S(1)} %fusion.6), channel_id=1, replica_groups=mesh['parts'=2,'seq'=4,'chan'=4] {'seq'}, dimensions={0}, use_global_device_ids=true | all-gather | bytes 163840 | tf_op jit(solution)/shard_map/all_gather | solution.py:48
  30.2 13.0 %fusion.2 = f32[32,3,2048]{2,0,1:T(8,128)} fusion(bf16[3,2048,2048]{2,1,0:T(8,128)(2,1)} %param.8, bf16[32,2048]{1,0:T(8,128)(2,1)S(1)} %all_gather.6), kind=kOutput, calls=%fused_computation.8 | convolution fusion | flops 805306368 | bytes 26083328 | tf_op jit(solution)/shard_map/dot_general | solution.py:35
  43.2 0.0 reduce-scatter.2.cloned.1.call-update
  43.3 0.8 slice_bitcast_fusion.10
  44.1 22.8 %reduce-scatter.2.cloned.1.call-done = f32[8,3,2048]{2,0,1:T(8,128)} async-done(((f32[32,3,2048]{2,0,1:T(8,128)}), f32[8,3,2048]{2,0,1:T(8,128)}) %reduce-scatter.2.cloned.1.call-update) | async-done | bytes 196624 | tf_op jit(solution)/shard_map/reduce_scatter | solution.py:51
  66.9 0.9 convert_element_type.20
  67.9 1.8 %collective-permute-start = (bf16[8,3,2048]{2,0,1:T(8,128)(2,1)S(1)}, bf16[8,3,2048]{2,0,1:T(8,128)(2,1)S(1)}, u32[]{:S(2)}, u32[]{:S(2)}) collective-permute-start(bf16[8,3,2048]{2,0,1:T(8,128)(2,1)S(1)} %convert_element_type.20), channel_id=1, source_target_pairs={{0,1},{1,2},{2,3},{4,5},{5,6},{6,7},{8,9},{9,10},{10,11},{12,13},{... | collective-permute-start | bytes 294920 | tf_op jit(solution)/shard_map/ppermute | solution.py:16
  69.6 0.9 slice_bitcast_fusion.17
  70.6 0.1 broadcast_in_dim.34
  70.7 0.1 broadcast_in_dim.35
  70.7 0.1 broadcast_in_dim.36
  70.8 0.1 broadcast_in_dim.37
  70.9 0.1 broadcast_in_dim.38
  71.0 0.1 broadcast_in_dim.39
  71.1 0.1 broadcast_in_dim.40
  71.2 0.1 broadcast_in_dim.41
  71.2 0.1 broadcast_in_dim.42
  71.3 0.1 broadcast_in_dim.43
  71.4 0.1 broadcast_in_dim.44
  71.5 0.1 broadcast_in_dim.45
  71.6 0.1 broadcast_in_dim.46
  71.7 0.1 broadcast_in_dim.47
  71.8 0.0 collective-permute-done
  71.8 0.1 fusion
  72.0 0.1 fusion.10
  72.0 13.6 %all_gather.7 = bf16[8,8192]{1,0:T(8,128)(2,1)S(1)} all-gather(bf16[8,2048]{1,0:T(8,128)(2,1)S(1)} %fusion.10), channel_id=1, replica_groups=mesh['parts'=2,'seq'=4,'chan'=4] {'seq'}, dimensions={1}, use_global_device_ids=true | all-gather | bytes 163840 | tf_op jit(solution)/shard_map/all_gather | solution.py:57
  85.7 15.1 %convolution_convert_fusion = bf16[8,2048]{1,0:T(8,128)(2,1)} fusion(bf16[8,8192]{1,0:T(8,128)(2,1)S(1)} %all_gather.7, bf16[2048,8192]{1,0:T(8,128)(2,1)} %param.11), kind=kOutput, calls=%fused_computation | convolution fusion | flops 268451840 | bytes 33718272 | tf_op jit(solution)/shard_map/dot_general | solution.py:35
  (3 shorter events, 0.1 us)
Async XLA Ops:
  6.5 60.4 %reduce-scatter.2.cloned.1.call-start = ((), (), s32[]{:S(2)}) async-start(), calls=%async_computation.1 | async-start | bytes 983040 | tf_op jit(solution)/shard_map/reduce_scatter | solution.py:51
  67.9 3.9 %collective-permute-start = (bf16[8,3,2048]{2,0,1:T(8,128)(2,1)S(1)}, bf16[8,3,2048]{2,0,1:T(8,128)(2,1)S(1)}, u32[]{:S(2)}, u32[]{:S(2)}) collective-permute-start(bf16[8,3,2048]{2,0,1:T(8,128)(2,1)S(1)} %convert_element_type.20), channel_id=1, source_target_pairs={{0,1},{1,2},{2,3},{4,5},{5,6},{6,7},{8,9},{9,10},{10,11},{12,13},{... | collective-permute-start | bytes 294920 | tf_op jit(solution)/shard_map/ppermute | solution.py:16
Sparse Core Ops, SparseCore 0:
  43.4 23.4 reduce-scatter.1
where the time goes:
time: 108 us
  blocking collectives  35.6 us (33%)
  matrix products  28.1 us (26%)
  waiting for transfers between devices  22.9 us (21%)
  between operations  13.4 us (12%)
  local copies, waits for them, and re-layouts  2.93 us (3%)
  other arithmetic  2.92 us (3%)
  starting transfers between devices  1.76 us (2%)
    dot_general x2, matrix products, contract_last(): lax.dot_general(left, right, (((1,), (1,)), ((), ())), preferred_element_...  28.1 us
    reduce_scatter x1, waiting for transfers between devices, shards(): lax.psum_scatter(partial_terms, 'chan', scatter_dimension=0, tiled=True)  22.8 us
    all_gather x1, blocking collectives, shards(): lax.all_gather(gated, 'seq', axis=1, tiled=True)  13.6 us
    all_gather x1, blocking collectives, shards(): piece = lax.all_gather(normed, 'seq', axis=0, tiled=True)  13.6 us
    psum x1, blocking collectives, shards(): total_squares = lax.psum(local_squares, 'chan')  8.34 us
  transfers between devices with their start and end apart: 2, of which 1 were waited for; matrix products, arithmetic and copies ran while one was open for 3% of the time, Pallas kernels for 0%

commit v1 on v0

--- a/solution.py
+++ b/solution.py
@@ -1,10 +1,15 @@
+import functools
+
 import jax
 import jax.numpy as jnp
 from jax import lax
+from jax.experimental import pallas as pl
+from jax.experimental.pallas import tpu as pltpu
 from jax.sharding import PartitionSpec as P
 
 D = 8192
 GROUP = 16
+MIB = 2**20
 
 
 epsilon = 1e-06
@@ -37,7 +42,7 @@
     )
 
 
-def shards(x_tokens, norm_gain, w_in, short_filter, se_filter, w_out):
+def plain(x_tokens, norm_gain, w_in, short_filter, se_filter, w_out):
     wide = x_tokens.astype(jnp.float32)
     local_squares = jnp.sum(wide * wide, axis=1, keepdims=True)
     total_squares = lax.psum(local_squares, "chan")
@@ -58,6 +63,226 @@
     return result.astype(jnp.bfloat16)
 
 
+def partners(me, count):
+    if count % 2:
+        return [lax.rem(me + step, count) for step in range(1, count)]
+    chip, core, chips = me // 2, lax.rem(me, 2), count // 2
+    found = []
+    for step in range(1, chips):
+        other = 2 * lax.rem(chip + step, chips)
+        found += [other + core, other + 1 - core]
+    return found + [2 * chip + 1 - core]
+
+
+def delayed(value, steps):
+    if steps == 0:
+        return value
+    tokens = lax.broadcasted_iota(jnp.int32, value.shape, 0)
+    return jnp.where(tokens >= steps, pltpu.roll(value, steps, 0), 0.0)
+
+
+def kernel(
+    seqs, chans,
+    x_hbm, gain_hbm, w_in_hbm, short_hbm, se_hbm, w_out_hbm, out_ref,
+    xs, gain, w_in, short, se, w_out, normed, squares, factors, stage, landed, own, gathered, total,
+    leaving, arriving,
+    small_sem, w_in_sem, w_out_sem, x_send, x_recv, sq_send, sq_recv, f_send, f_recv, p_send, p_recv,
+    g_send, g_recv, o_send, o_recv,
+):
+    seq, chan = lax.axis_index("seq"), lax.axis_index("chan")
+    tokens, block = own.shape[1:]
+    columns, features = w_out.shape[1], w_in.shape[3]
+    rows = out_ref.shape[0]
+    seq_others = [lax.rem(seq + step, seqs) for step in range(1, seqs)]
+    chan_others = partners(chan, chans)
+
+    def send(source, target, send_sem, recv_sem, axis, index):
+        copy = pltpu.make_async_remote_copy(
+            src_ref=source, dst_ref=target, send_sem=send_sem, recv_sem=recv_sem,
+            device_id={axis: index}, device_id_type=pl.DeviceIdType.MESH,
+        )
+        copy.start()
+        return copy
+
+    def local(source, target, sem):
+        copy = pltpu.make_async_copy(source, target, sem)
+        copy.start()
+        return copy
+
+    def arrived(target, sem):
+        pltpu.make_async_copy(target, target, sem).wait()
+
+    x_copy = local(x_hbm, xs.at[seq], small_sem.at[0])
+    gain_copy = local(gain_hbm, gain, small_sem.at[1])
+    short_copy = local(short_hbm, short, small_sem.at[2])
+    se_copy = local(se_hbm, se, small_sem.at[3])
+    w_in_copies = []
+    for step, index in enumerate(chan_others + [chan]):
+        span = pl.ds(pl.multiple_of(index * block, block), block)
+        w_in_copies.append([
+            local(w_in_hbm.at[part, span], w_in.at[step, part], w_in_sem.at[step, part])
+            for part in range(3)
+        ])
+    w_out_copies = []
+    for step, index in enumerate([seq] + seq_others):
+        span = pl.ds(pl.multiple_of(index * columns + chan * block, block), block)
+        w_out_copies.append(local(w_out_hbm.at[:, span], w_out.at[step], w_out_sem.at[step]))
+
+    barrier = pltpu.get_barrier_semaphore()
+    for axis, others in (("seq", seq_others), ("chan", chan_others)):
+        for index in others:
+            pl.semaphore_signal(
+                barrier, inc=1, device_id={axis: index}, device_id_type=pl.DeviceIdType.MESH
+            )
+    x_copy.wait()
+    pl.semaphore_wait(barrier, seqs + chans - 2)
+
+    sent = [
+        send(xs.at[seq], xs.at[seq], x_send.at[step], x_recv.at[seq], "seq", index)
+        for step, index in enumerate(seq_others)
+    ]
+
+    wide = xs[seq].astype(jnp.float32)
+    squares[chan] = jnp.broadcast_to(
+        jnp.sum(wide * wide, axis=1, keepdims=True), squares.shape[1:]
+    )
+    sent += [
+        send(squares.at[chan], squares.at[chan], sq_send.at[step], sq_recv.at[chan], "chan", index)
+        for step, index in enumerate(chan_others)
+    ]
+    for index in chan_others:
+        arrived(squares.at[index], sq_recv.at[index])
+    factors[seq] = lax.rsqrt(jnp.sum(squares[...], axis=0) / (features * chans) + epsilon)
+    sent += [
+        send(factors.at[seq], factors.at[seq], f_send.at[step], f_recv.at[seq], "seq", index)
+        for step, index in enumerate(seq_others)
+    ]
+
+    se_copy.wait()
+    short_copy.wait()
+    gain_copy.wait()
+    filters = se.shape[1]
+    group = columns // filters
+    first = lax.broadcasted_iota(jnp.int32, (filters, block), 0) * group
+    channel = lax.broadcasted_iota(jnp.int32, (filters, block), 1) + chan * block
+    spread = jnp.where((channel >= first) & (channel < first + group), 1.0, 0.0)
+    long_taps = jnp.dot(
+        se[...], spread, preferred_element_type=jnp.float32, precision=lax.Precision.HIGHEST
+    )
+
+    for index in seq_others:
+        arrived(factors.at[index], f_recv.at[index])
+        arrived(xs.at[index], x_recv.at[index])
+    wide = xs[...].astype(jnp.float32).reshape(tokens, features)
+    factor = factors[...].reshape(tokens, 128)[:, :1]
+    normed[...] = (wide * factor * gain[...]).astype(jnp.bfloat16)
+
+    for step in range(chans):
+        for part in range(3):
+            w_in_copies[step][part].wait()
+            terms = contract_last(normed[...], w_in[step, part])
+            if step == chans - 1:
+                own[part] = terms
+                continue
+            stage[step, part] = terms.astype(jnp.bfloat16)
+            sent.append(send(
+                stage.at[step, part], landed.at[chan, part],
+                p_send.at[step, part], p_recv.at[chan, part], "chan", chan_others[step],
+            ))
+
+    mine = pl.ds(pl.multiple_of(chan * block, block), block)
+    featured = []
+    for part in range(3):
+        value = own[part]
+        for index in reversed(chan_others):
+            arrived(landed.at[index, part], p_recv.at[index, part])
+            value += landed[index, part].astype(jnp.float32)
+        featured.append(sum(
+            short[lag, part : part + 1, mine] * delayed(value, lag) for lag in range(3)
+        ))
+    product = featured[1] * featured[2]
+    filtered = sum(long_taps[lag : lag + 1] * delayed(product, lag) for lag in range(7))
+    gathered[seq] = (featured[0] * filtered).astype(jnp.bfloat16)
+    sent += [
+        send(gathered.at[seq], gathered.at[seq], g_send.at[step], g_recv.at[seq], "seq", index)
+        for step, index in enumerate(seq_others)
+    ]
+
+    for step, index in enumerate([seq] + seq_others):
+        w_out_copies[step].wait()
+        if step > 0:
+            arrived(gathered.at[index], g_recv.at[index])
+        terms = contract_last(gathered[index], w_out[step])
+        if step == 0:
+            total[...] = terms
+        else:
+            total[...] += terms
+    leaving[...] = total[...].reshape(leaving.shape).astype(jnp.bfloat16)
+    sent += [
+        send(leaving.at[index], arriving.at[chan], o_send.at[step], o_recv.at[chan], "chan", index)
+        for step, index in enumerate(chan_others)
+    ]
+    result = total[pl.ds(pl.multiple_of(chan * rows, rows), rows)]
+    for index in reversed(chan_others):
+        arrived(arriving.at[index], o_recv.at[index])
+        result += arriving[index].astype(jnp.float32)
+    out_ref[...] = result.astype(jnp.bfloat16)
+    for copy in sent:
+        copy.wait_send()
+
+
+def shards(seqs, chans, x_tokens, norm_gain, w_in, short_filter, se_filter, w_out):
+    held, features = x_tokens.shape
+    columns = w_in.shape[1]
+    tokens, block, rows = held * seqs, columns // chans, held * seqs // chans
+    weight_bytes = 2 * (w_in.size + w_out.size // chans)
+    if (
+        seqs < 2 or chans < 2 or held % 8 or rows % 8 or tokens != rows * chans or tokens > 256
+        or block * chans != columns or block % 128 or features % 128 or weight_bytes > 40 * MIB
+    ):
+        return plain(x_tokens, norm_gain, w_in, short_filter, se_filter, w_out)
+    bf16, f32 = jnp.bfloat16, jnp.float32
+    dma = pltpu.SemaphoreType.DMA
+    anywhere = pl.BlockSpec(memory_space=pl.ANY)
+    return pl.pallas_call(
+        functools.partial(kernel, seqs, chans),
+        out_shape=jax.ShapeDtypeStruct((rows, columns), bf16),
+        in_specs=[anywhere] * 6,
+        out_specs=pl.BlockSpec(memory_space=pltpu.VMEM),
+        scratch_shapes=[
+            pltpu.VMEM((seqs, held, features), bf16),
+            pltpu.VMEM((1, features), f32),
+            pltpu.VMEM((chans, 3, block, features), bf16),
+            pltpu.VMEM(short_filter.shape, f32),
+            pltpu.VMEM(se_filter.shape, f32),
+            pltpu.VMEM((seqs, columns, block), bf16),
+            pltpu.VMEM((tokens, features), bf16),
+            pltpu.VMEM((chans, held, 128), f32),
+            pltpu.VMEM((seqs, held, 128), f32),
+            pltpu.VMEM((chans - 1, 3, tokens, block), bf16),
+            pltpu.VMEM((chans, 3, tokens, block), bf16),
+            pltpu.VMEM((3, tokens, block), f32),
+            pltpu.VMEM((seqs, tokens, block), bf16),
+            pltpu.VMEM((tokens, columns), f32),
+            pltpu.VMEM((chans, rows, columns), bf16),
+            pltpu.VMEM((chans, rows, columns), bf16),
+            dma((4,)), dma((chans, 3)), dma((seqs,)),
+            dma((seqs - 1,)), dma((seqs,)),
+            dma((chans - 1,)), dma((chans,)),
+            dma((seqs - 1,)), dma((seqs,)),
+            dma((chans - 1, 3)), dma((chans, 3)),
+            dma((seqs - 1,)), dma((seqs,)),
+            dma((chans - 1,)), dma((chans,)),
+        ],
+        compiler_params=pltpu.CompilerParams(
+            collective_id=0, has_side_effects=True, vmem_limit_bytes=52 * MIB
+        ),
+        cost_estimate=pl.CostEstimate(
+            flops=tokens * weight_bytes, bytes_accessed=weight_bytes, transcendentals=0
+        ),
+    )(x_tokens, norm_gain.reshape(1, features), w_in, short_filter, se_filter, w_out)
+
+
 def solution(mesh):
     placed = (
         P(("parts", "seq"), "chan"),
@@ -68,5 +293,6 @@
         P("seq", None),
     )
     return jax.shard_map(
-        shards, mesh=mesh, in_specs=placed, out_specs=P(("parts", "chan"), "seq"), check_vma=False
-    )
+        functools.partial(shards, mesh.shape["seq"], mesh.shape["chan"]),
+        mesh=mesh, in_specs=placed, out_specs=P(("parts", "chan"), "seq"), check_vma=False,
+    )

time: 108 us -> 32.6 us (0.30)
  blocking collectives: 35.6 us -> 0 us
  Pallas kernels: 0 us -> 28.6 us
  matrix products: 28.1 us -> 0 us
  waiting for transfers between devices: 22.9 us -> 0 us
  between operations: 13.4 us -> 0.01 us
  other arithmetic: 2.92 us -> 0 us
  starting transfers between devices: 1.76 us -> 0 us
    pallas_call x0 -> x1, Pallas kernels: none -> 28.6 us  [shards(): pl.pallas_call(functools.partial(kernel, seqs, chans), out_shape=jax.Shap...]
    dot_general x2 -> x0, matrix products: 28.1 us -> none  [contract_last(): lax.dot_general(left, right, (((1,), (1,)), ((), ())), preferred_element_...]
    all_gather x2 -> x0, blocking collectives: 27.2 us -> none  [the longest x1 13.6 us: shards(): lax.all_gather(gated, 'seq', axis=1, tiled=True)]
    reduce_scatter x1 -> x0, waiting for transfers between devices: 22.8 us -> none  [shards(): lax.psum_scatter(partial_terms, 'chan', scatter_dimension=0, tiled=True)]
    psum x1 -> x0, blocking collectives: 8.34 us -> none  [shards(): total_squares = lax.psum(local_squares, 'chan')]
    unnamed x0 -> x9, local copies, waits for them, and re-layouts: none -> 3.65 us
    convert_element_type x4 -> x0, other arithmetic: 1.88 us -> none  [the longest x1 0.94 us: shards(): lax.psum_scatter(partial_terms, 'chan', scatter_dimension=0, tiled=True)]
    ppermute x1 -> x0, starting transfers between devices: 1.76 us -> none  [from_behind(): lax.ppermute(value, axis, [(source, source + steps) for source in range(l...]
  transfers between devices with their start and end apart: 2 -> 0, of which waited for: 1 -> 0; matrix products, arithmetic and copies ran while one was open for 3% -> 0% of each run, Pallas kernels for 0% -> 0%
where the time goes in v1:
time: 32.6 us; the launch traced here: 32.3 us
  Pallas kernels  28.6 us (88%)
  local copies, waits for them, and re-layouts  3.65 us (11%)
    pallas_call x1, Pallas kernels, shards(): pl.pallas_call(functools.partial(kernel, seqs, chans), out_shape=jax.Shap...  28.6 us
    unnamed x9, local copies, waits for them, and re-layouts  3.65 us

profile of v1, /device:TPU:0, one launch (start us, length us, event | category | flops | bytes accessed | tf_op | source)
XLA Modules:
  0.0 32.3 jit_solution(11146464923113384075)
XLA Ops:
  0.0 0.0 copy-start
  0.0 0.9 %copy-done = f32[3,3,2048]{2,1,0:T(4,128)S(1)} copy-done((f32[3,3,2048]{2,1,0:T(4,128)S(1)}, f32[3,3,2048]{2,1,0:T(4,128)}, u32[]{:S(2)}) %copy-start) | copy-done | bytes 73752
  0.9 0.0 copy-start.1
  0.9 0.8 %copy-done.1 = bf16[8,2048]{1,0:T(8,128)(2,1)S(1)} copy-done((bf16[8,2048]{1,0:T(8,128)(2,1)S(1)}, bf16[8,2048]{1,0:T(8,128)(2,1)}, u32[]{:S(2)}) %copy-start.1) | copy-done | bytes 32792
  1.7 0.0 copy-start.2
  1.7 0.7 %copy-done.2 = f32[2048]{0:T(1024)S(1)} copy-done((f32[2048]{0:T(1024)S(1)}, f32[2048]{0:T(1024)}, u32[]{:S(2)}) %copy-start.2) | copy-done | bytes 8216
  2.3 0.0 copy-start.3
  2.4 0.7 %copy-done.3 = f32[7,128]{1,0:T(8,128)S(1)} copy-done((f32[7,128]{1,0:T(8,128)S(1)}, f32[7,128]{1,0:T(8,128)}, u32[]{:S(2)}) %copy-start.3) | copy-done | bytes 3608
  3.0 28.6 %shard_map.64 = bf16[8,2048]{1,0:T(8,128)(2,1)S(1)} custom-call(bf16[8,2048]{1,0:T(8,128)(2,1)S(1)} %copy-done.1, f32[1,2048]{1,0:T(1,128)S(1)} %bitcast.1, bf16[3,2048,2048]{2,1,0:T(8,128)(2,1)} %w_in_hbm.1, f32[3,3,2048]{2,1,0:T(4,128)S(1)} %copy-done, f32[7,128]{1,0:T(8,128)S(1)} %copy-done.3, bf16[2048,8192]{1,0:T(8,128)(2,1)} %w_out_hbm.1), custom_call_target="tpu_custom_call" | custom-call | flops 1073741824 | bytes 33554432 | tf_op jit(solution)/shard_map/pallas_call | solution.py:247
  31.7 0.6 %copy.8 = bf16[8,2048]{1,0:T(8,128)(2,1)} copy(bf16[8,2048]{1,0:T(8,128)(2,1)S(1)} %shard_map.64) | data formatting | bytes 65536
Async XLA Ops:
  0.0 0.9 %copy-start = (f32[3,3,2048]{2,1,0:T(4,128)S(1)}, f32[3,3,2048]{2,1,0:T(4,128)}, u32[]{:S(2)}) copy-start(f32[3,3,2048]{2,1,0:T(4,128)} %short_hbm.1) | copy-start | bytes 221188
  0.9 0.8 %copy-start.1 = (bf16[8,2048]{1,0:T(8,128)(2,1)S(1)}, bf16[8,2048]{1,0:T(8,128)(2,1)}, u32[]{:S(2)}) copy-start(bf16[8,2048]{1,0:T(8,128)(2,1)} %x_hbm.1) | copy-start | bytes 98308
  1.7 0.7 %copy-start.2 = (f32[2048]{0:T(1024)S(1)}, f32[2048]{0:T(1024)}, u32[]{:S(2)}) copy-start(f32[2048]{0:T(1024)} %param.7) | copy-start | bytes 24580
  2.3 0.7 %copy-start.3 = (f32[7,128]{1,0:T(8,128)S(1)}, f32[7,128]{1,0:T(8,128)}, u32[]{:S(2)}) copy-start(f32[7,128]{1,0:T(8,128)} %se_hbm.1) | copy-start | bytes 10756
